TPU v7x, 1024 devices: a whole 8x8x8 slice. The times are simulated.
1024 devices in a mesh: sens: 64 (over z_hi, x, core), pts: 16 (over y, z_lo).
Axes of the slice: x: 8, y: 8, z: 8 (z_hi: 4, z_lo: 2; z = z_hi * 2 + z_lo), core: 2. Of those that a mesh axis runs over, the one named last changes fastest.
Arguments:
- observed: float32 [128, 2, 420], P('sens'), may hold values from -8 to 8
- spectra: bfloat16 [2, 211, 128, 12288], P(None, None, 'sens', 'pts'), may hold values from -1 to 1
- prior_factor: bfloat16 [12288, 768], P('pts'), may hold values from -0.21875 to 0.21875
- noise_cov: bfloat16 [4, 420, 420], replicated, may hold values from -1 to 1.25
- noise_inv: bfloat16 [4, 420, 420], replicated, may hold values from -1 to 1.25
- sensor_block: int32 [128], P('sens'), may hold values from 0 to 3
- window_len: int32 [128], P('sens'), may hold values from 105 to 420, as said below
Outputs:
- solution: float32 [128, 2, 420], P('sens')
- residual: float32 [128, 2, 420], P('sens')
Inputs may be any that keep to these rules, and one draw needn't show every extreme that they name: `window_len`: some sensor has all 420 samples active.
All inputs are finite; a program needn't handle non-finite values.
Results may differ from a plain program's by a relative error of at most 0.012.
The roundings to bfloat16 on the way count: a program that leaves them out, or rounds other values in their place, can miss the bound.
Values may be sent and summed in bfloat16 or wider, within the bound.
A program may use at most 64 MiB of HBM per device.

v0:
```python
import math

import jax
import jax.numpy as jnp
from jax import lax
from jax.sharding import PartitionSpec as P


def apply_table(matrix_set, field_in, sensor_block):
    tables = matrix_set[sensor_block].astype(jnp.float32)
    return jnp.einsum("stu,sru->srt", tables, field_in, precision=lax.Precision.HIGHEST)


def shards(observed, spectra, prior_factor, noise_cov, noise_inv, sensor_block, window_len):
    count_sens, count_rhs, count_time = observed.shape
    count_bins = count_time // 2 + 1
    time_index = jnp.arange(count_time, dtype=jnp.int32)
    bin_index = jnp.arange(count_bins, dtype=jnp.int32)
    window_mask = (time_index[None, :] < window_len[:, None]).astype(jnp.float32)
    start_res = observed * window_mask[:, None, :]
    direction = window_mask[:, None, :] * apply_table(noise_inv, start_res, sensor_block)
    inner_local = jnp.sum(start_res * direction, axis=(0, 2))
    cov_image = window_mask[:, None, :] * apply_table(noise_cov, direction, sensor_block)
    phases = time_index[:, None] * bin_index[None, :] % count_time
    angles = phases.astype(jnp.float32) * (2.0 * math.pi / count_time)
    cosine = jnp.cos(angles)
    sine_pos = jnp.where(phases % (count_time // 2) == 0, 0.0, jnp.sin(angles))
    flat_dir = direction.reshape(-1, count_time)
    hat_re = (
        jnp.dot(flat_dir, cosine, precision=lax.Precision.HIGHEST)
        .reshape(count_sens, count_rhs, count_bins)
        .astype(jnp.bfloat16)
    )
    hat_im = (
        jnp.dot(flat_dir, -sine_pos, precision=lax.Precision.HIGHEST)
        .reshape(count_sens, count_rhs, count_bins)
        .astype(jnp.bfloat16)
    )
    bin_weight = (
        jnp.where((bin_index == 0) | (2 * bin_index == count_time), 1.0, 2.0).astype(jnp.float32)
        / count_time
    )
    inner_total = lax.psum(inner_local, "sens")
    spec_re = spectra[0]
    spec_im = spectra[1]
    part_re = jnp.einsum(
        "fsp,srf->frp", spec_re, hat_re, preferred_element_type=jnp.float32
    ) + jnp.einsum("fsp,srf->frp", spec_im, hat_im, preferred_element_type=jnp.float32)
    part_im = jnp.einsum(
        "fsp,srf->frp", spec_re, hat_im, preferred_element_type=jnp.float32
    ) - jnp.einsum("fsp,srf->frp", spec_im, hat_re, preferred_element_type=jnp.float32)
    partial_adj = jnp.stack([part_re, part_im])
    share_adj = lax.psum_scatter(partial_adj, "sens", scatter_dimension=3, tiled=True).astype(
        jnp.bfloat16
    )
    adjoint = lax.all_gather(share_adj, "sens", axis=3, tiled=True)
    weighted = jnp.einsum(
        "xfrp,pq->xfrq", adjoint, prior_factor, preferred_element_type=jnp.float32
    )
    spread = jnp.einsum(
        "xfrq,pq->xfrp",
        weighted.astype(jnp.bfloat16),
        prior_factor,
        preferred_element_type=jnp.float32,
    ).astype(jnp.bfloat16)
    out_re = jnp.einsum(
        "fsp,frp->srf", spec_re, spread[0], preferred_element_type=jnp.float32
    ) - jnp.einsum("fsp,frp->srf", spec_im, spread[1], preferred_element_type=jnp.float32)
    out_im = jnp.einsum(
        "fsp,frp->srf", spec_re, spread[1], preferred_element_type=jnp.float32
    ) + jnp.einsum("fsp,frp->srf", spec_im, spread[0], preferred_element_type=jnp.float32)
    total_fwd = lax.psum(jnp.stack([out_re, out_im]), "pts")
    inv_cos = (cosine * bin_weight[None, :]).T
    inv_sin = (sine_pos * bin_weight[None, :]).T
    signal = jnp.dot(
        total_fwd[0].reshape(-1, count_bins), inv_cos, precision=lax.Precision.HIGHEST
    ) - jnp.dot(total_fwd[1].reshape(-1, count_bins), inv_sin, precision=lax.Precision.HIGHEST)
    signal = signal.reshape(count_sens, count_rhs, count_time)
    image = cov_image + window_mask[:, None, :] * signal
    curvature = lax.psum(jnp.sum(direction * image, axis=(0, 2)), "sens")
    step_size = inner_total / curvature
    solution = step_size[None, :, None] * direction
    residual = start_res - step_size[None, :, None] * image
    return (solution, residual)


def solution(mesh):
    placed = (
        P("sens", None, None),
        P(None, None, "sens", "pts"),
        P("pts", None),
        P(),
        P(),
        P("sens"),
        P("sens"),
    )
    return jax.shard_map(
        shards,
        mesh=mesh,
        in_specs=placed,
        out_specs=(P("sens", None, None), P("sens", None, None)),
        check_vma=False,
    )
```

profile of v0, /device:TPU:1, one launch (start us, length us, event | category | flops | bytes accessed | tf_op | source)
XLA Modules:
  0.0 660.3 jit_solution(17564475044375194093)
XLA Ops:
  7.2 0.0 copy-start
  7.2 0.0 all-gather.2.cloned.1.call-start
  7.2 0.8 compare_convert_fusion
  8.1 0.7 compare_select_fusion
  8.7 0.0 copy-done
  8.7 0.0 copy-start.9
  8.8 7.1 %gather_fusion = bf16[2,420,420]{2,0,1:T(2,128)(2,1)S(1)} fusion(bf16[4,420,420]{2,0,1:T(4,128)(2,1)S(1)} %copy-done, s32[1024]{0:T(1024)S(1)} %pad_clamp_fusion), kind=kCustom, calls=%fused_computation | custom fusion | bytes 1411208 | tf_op jit(solution)/shard_map/gather | solution.py:10
  15.9 0.0 copy-done.9
  15.9 0.8 convolution_multiply_fusion
  16.6 2.3 convolution_convert_fusion.3
  19.0 2.5 convolution_convert_fusion.2
  21.5 0.2 copy.33
  21.7 1.5 slice_bitcast_fusion.3
  23.3 0.0 copy-start.5
  23.3 0.2 copy.34
  23.5 0.8 fusion.65
  24.3 0.0 copy-done.5
  24.3 0.0 copy-start.7
  24.3 0.8 fusion.66
  25.1 0.5 copy-done.7
  25.6 0.9 fusion.2
  26.5 0.9 fusion.1
  27.5 2.7 pad_maximum_fusion
  30.2 6.7 %copy.37 = f32[2,211,2,768]{1,2,0,3:T(2,128)} copy(f32[2,211,2,768]{3,2,1,0:T(2,128)} %pad_maximum_fusion) | data formatting | bytes 5185536 | tf_op jit(solution)/shard_map/stack | solution.py:52
  36.9 0.0 copy-start.1
  36.9 327.0 %all-reduce.3 = bf16[2,211,2,768]{1,2,0,3:T(2,128)(2,1)} all-reduce(f32[2,211,2,768]{1,2,0,3:T(2,128)} %copy.37), channel_id=2, replica_groups=mesh['sens'=64,'pts'=16] {'sens'}, use_global_device_ids=true, to_apply=%region_2.3.clone | all-reduce | flops 648192 | bytes 3889152
  363.9 1.3 dynamic-slice
  365.8 1.4 dynamic-slice_convert_fusion
  367.2 0.0 all-gather.2.cloned.1.call-update
  367.2 0.0 copy-done.1
  367.2 8.0 %gather_fusion.1 = bf16[2,420,420]{2,0,1:T(2,128)(2,1)} fusion(bf16[4,420,420]{2,0,1:T(4,128)(2,1)S(1)} %copy-done.1, s32[1024]{0:T(1024)S(1)} %pad_clamp_fusion), kind=kCustom, calls=%fused_computation.1 | custom fusion | bytes 1411208 | tf_op jit(solution)/shard_map/gather | solution.py:10
  375.2 86.5 %all-gather.2.cloned.1.call-done = bf16[2,211,2,768]{1,2,0,3:T(2,128)(2,1)} async-done(((bf16[2,211,2,12]{1,2,0,3:T(2,128)(2,1)}), bf16[2,211,2,768]{1,2,0,3:T(2,128)(2,1)}) %all-gather.2.cloned.1.call-update) | async-done | bytes 1296400 | tf_op jit(solution)/shard_map/all_gather | solution.py:56
  461.7 4.8 convolution_convert_fusion
  466.5 0.0 copy-start.6
  466.5 0.1 slice_bitcast_fusion.1
  466.6 0.0 copy-start.3
  466.7 1.2 copy-done.6
  467.8 1.5 fusion.35
  469.4 0.0 copy-done.3
  469.4 0.0 copy-start.8
  469.4 1.6 fusion.31
  470.9 0.0 copy-done.8
  470.9 0.0 copy-start.4
  470.9 1.8 fusion.6
  472.8 0.1 copy.43
  472.9 0.0 copy-done.4
  472.9 1.9 fusion.5
  474.8 0.1 copy.44
  475.0 27.2 %psum.22 = f32[2,2,2,211]{3,2,1,0:T(2,128)S(1)} all-reduce(f32[2,2,2,211]{3,2,1,0:T(2,128)S(1)} %pad_maximum_fusion.1), channel_id=1, replica_groups=mesh['sens'=64,'pts'=16] {'pts'}, use_global_device_ids=true, to_apply=%region_3.4 | all-reduce | flops 1688 | bytes 13504 | tf_op jit(solution)/shard_map/psum | solution.py:72
  502.2 2.1 fusion.18
  504.3 0.0 copy-start.2
  504.3 2.5 convolution_subtract_fusion.2
  506.8 0.1 reshape.43
  506.8 0.0 copy-done.2
  506.9 0.9 multiply_reduce_fusion
  507.8 145.0 %all-reduce.1 = (f32[2]{0:T(128)S(1)}, f32[2]{0:T(128)S(1)}) all-reduce(f32[2]{0:T(128)S(1)} %get-tuple-element.3, f32[2]{0:T(128)S(1)} %get-tuple-element.2), channel_id=1, replica_groups=mesh['sens'=64,'pts'=16] {'sens'}, use_global_device_ids=true, to_apply=%region_1.2 | all-reduce | flops 4 | bytes 32 | tf_op jit(solution)/shard_map/psum | solution.py:43
  652.8 0.7 multiply_subtract_fusion
  (7 shorter events, 0.1 us)
Async XLA Ops:
  7.2 1.6 copy-start
  7.2 454.5 %all-gather.2.cloned.1.call-start = ((), (), s32[]{:S(2)}) async-start(), calls=%async_computation | async-start | bytes 1597440 | tf_op jit(solution)/shard_map/all_gather | solution.py:56
  8.7 7.1 %copy-start.9 = (f32[2,2,420]{2,1,0:T(2,128)S(1)}, f32[2,2,420]{2,1,0:T(2,128)}, u32[]{:S(2)}) copy-start(f32[2,2,420]{2,1,0:T(2,128)} %param.7) | copy-start | bytes 20164
  23.3 1.0 copy-start.5
  24.3 1.3 copy-start.7
  36.9 330.3 %copy-start.1 = (bf16[4,420,420]{2,0,1:T(4,128)(2,1)S(1)}, bf16[4,420,420]{2,0,1:T(4,128)(2,1)}, u32[]{:S(2)}) copy-start(bf16[4,420,420]{2,0,1:T(4,128)(2,1)} %param.10) | copy-start | bytes 4233604
  466.5 1.3 copy-start.6
  466.6 2.7 copy-start.3
  469.4 1.6 copy-start.8
  470.9 2.0 copy-start.4
  504.3 2.5 copy-start.2
Sparse Core Ops, SparseCore 0:
  367.3 94.3 all-gather.1
where the time goes:
time: 661 us; the launch traced here: 660 us
  blocking collectives  499 us (75%)
  waiting for transfers between devices  86.5 us (13%)
  local copies, waits for them, and re-layouts  28.4 us (4%)
  matrix products  26.3 us (4%)
  between operations  14.9 us (2%)
    unnamed x1, blocking collectives  327 us
    psum x1, blocking collectives, shards(): inner_total = lax.psum(inner_local, 'sens')  145 us
    all_gather x1, waiting for transfers between devices, shards(): adjoint = lax.all_gather(share_adj, 'sens', axis=3, tiled=True)  86.5 us
    psum x1, blocking collectives, shards(): total_fwd = lax.psum(jnp.stack([out_re, out_im]), 'pts')  27.2 us
    gather x2, local copies, waits for them, and re-layouts, apply_table(): tables = matrix_set[sensor_block].astype(jnp.float32)  15.1 us
  transfers between devices with their start and end apart: 1, of which 1 were waited for; matrix products, arithmetic and copies ran while one was open for 1% of the time, Pallas kernels for 0%

commit v1 on v0

v1 whole, which is shorter than its diff:
```python
import functools
import math

import jax
import jax.numpy as jnp
import numpy as np
from jax import lax
from jax.experimental import pallas as pl
from jax.experimental.pallas import tpu as pltpu
from jax.sharding import PartitionSpec as P

MESH = pl.DeviceIdType.MESH
NT, F, PD, NB = 420, 211, 768, 4
NS, NP = 64, 16
FB = 4
NC = -(-F // FB)
TP = 432
FIRST = 40
f32, bf16 = jnp.float32, jnp.bfloat16


def chunk_of(dev):
    return (dev * NC + NS - 1) // NS


def is_owner(dev):
    c = chunk_of(dev)
    return (c * NS) // NC == dev


@functools.cache
def tables():
    t = np.arange(NT)
    fwd = np.zeros((2, FB, NS, NT))
    inv = np.zeros((NS, 2, FB, NT))
    for dev in range(NS):
        c = -(-dev * NC // NS)
        if (c * NS) // NC != dev or c >= NC:
            continue
        for f in range(FB):
            bin_ = FB * c + f
            if bin_ >= F:
                continue
            phase = (t * bin_) % NT
            cosine = np.cos(2 * math.pi * phase / NT)
            sine = np.where(phase % (NT // 2) == 0, 0.0, np.sin(2 * math.pi * phase / NT))
            weight = (1.0 if bin_ in (0, NT // 2) else 2.0) / NT
            fwd[0, f, dev], fwd[1, f, dev] = cosine, -sine
            inv[dev, 0, f], inv[dev, 1, f] = cosine * weight, -sine * weight
    fwd = fwd.reshape(2 * FB * NS, NT)
    inv = inv.reshape(4, 16, 8, NT).transpose(0, 2, 1, 3).reshape(512, NT)
    gt = np.zeros((128, 16))
    mask = np.zeros((16, 128))
    for xk in range(2):
        for x in range(2):
            for f in range(FB):
                for s in range(2):
                    mask[xk * 8 + f * 2 + s, xk * 32 + x * 16 + f * 4 + s * 2 :][:2] = 1
                    for r in range(2):
                        m = xk * 32 + x * 16 + f * 4 + s * 2 + r
                        j = f * 4 + (x if xk == 0 else 1 - x) * 2 + r
                        gt[m, j] = 1 if xk == 0 or x == 1 else -1
    rep = np.tile(np.eye(16), (1, 32))
    pick = np.zeros((128, 512))
    for row in range(128):
        pick[row, (row // 4) * 16 : (row // 4) * 16 + 16] = 1
    fold = np.zeros((8, 128))
    for row in range(128):
        fold[row % 4, row] = 1
    return dict(
        fwd=fwd.astype(np.float32),
        inv=inv.astype(np.float32),
        gt=gt.astype(np.float32),
        g=gt.T.astype(np.float32),
        mask=mask.astype(np.float32),
        rep=rep.astype(np.float32),
        pick=pick.astype(np.float32),
        fold=fold.astype(np.float32),
    )


def parts3(x):
    a = x.astype(bf16).astype(f32)
    b = (x - a).astype(bf16).astype(f32)
    return a, b, x - a - b


def parts2(x):
    a = x.astype(bf16)
    return a, (x - a.astype(f32)).astype(bf16)


def nt_dot(a, b):
    return lax.dot_general(a, b, (((1,), (1,)), ((), ())), preferred_element_type=f32)


def kernel(
    wl, sb, obs, kx, prior, ninv, ncov, dft, idft, gt, g, mask16, rep, pick, fold,
    sol, res,
    kk, prior_v, ninv_v, ncov_v, dft_v, idft_v, tsel, hsend, hrecv, vsend, vrecv, psend, precv, otmp,
    lsem, ksend, krecv, hss, hrs, vss, vrs, pss, prs,
):
    me, mp = lax.axis_index("sens"), lax.axis_index("pts")
    mine = is_owner(me)
    my_chunk = chunk_of(me)

    locals_ = [
        pltpu.make_async_copy(ninv, ninv_v.at[pl.ds(0, NT)], lsem.at[0]),
        pltpu.make_async_copy(dft, dft_v, lsem.at[1]),
        pltpu.make_async_copy(ncov, ncov_v.at[pl.ds(0, NT)], lsem.at[2]),
        pltpu.make_async_copy(prior, prior_v, lsem.at[3]),
        pltpu.make_async_copy(idft, idft_v, lsem.at[4]),
    ]
    for copy in locals_:
        copy.start()

    barrier = pltpu.get_barrier_semaphore()

    @pl.loop(1, NS)
    def _(k):
        pl.semaphore_signal(barrier, inc=1, device_id={"sens": lax.rem(me + k, NS)}, device_id_type=MESH)

    @pl.loop(1, NP)
    def _(k):
        pl.semaphore_signal(barrier, inc=1, device_id={"pts": lax.rem(mp + k, NP)}, device_id_type=MESH)

    pl.semaphore_wait(barrier, NS + NP - 2)

    def k_copy(peer):
        return pltpu.make_async_remote_copy(
            src_ref=kx.at[jnp.minimum(chunk_of(peer), NC - 1)],
            dst_ref=kk.at[pl.ds(pl.multiple_of(me * 16, 16), 16)],
            send_sem=ksend.at[peer],
            recv_sem=krecv.at[me],
            device_id={"sens": peer},
            device_id_type=MESH,
        )

    def k_arrived(peer):
        return pltpu.make_async_copy(
            kx.at[0], kk.at[pl.ds(pl.multiple_of(peer * 16, 16), 16)], krecv.at[peer]
        )

    def row_copy(src, dst, ss, rs, peer):
        return pltpu.make_async_remote_copy(
            src_ref=src.at[peer],
            dst_ref=dst.at[me],
            send_sem=ss.at[peer],
            recv_sem=rs.at[me],
            device_id={"sens": peer},
            device_id_type=MESH,
        )

    def row_arrived(src, dst, rs, peer):
        return pltpu.make_async_copy(src.at[peer], dst.at[peer], rs.at[peer])

    def start_k(k):
        peer = lax.rem(me + k, NS)

        @pl.when(is_owner(peer))
        def _():
            k_copy(peer).start()

    own = pltpu.make_async_copy(
        kx.at[jnp.minimum(my_chunk, NC - 1)], kk.at[pl.ds(pl.multiple_of(me * 16, 16), 16)], krecv.at[me]
    )

    @pl.when(mine)
    def _():
        own.start()

    pl.loop(1, FIRST)(start_k)

    time = lax.broadcasted_iota(jnp.int32, (2, NT), 1)
    masks = [(time < wl[s]).astype(f32) for s in range(2)]
    start = [obs[s] * masks[s] for s in range(2)]

    def select(table_v):
        @pl.loop(0, TP // 16)
        def _(i):
            rows = pl.ds(pl.multiple_of(i * 16, 16), 16)
            block = table_v[rows].astype(f32)
            which = lax.broadcasted_iota(jnp.int32, block.shape, 1)
            for s in range(2):
                tsel[s, rows, :] = jnp.where(which == sb[s], block, 0.0).sum(axis=1).astype(bf16)

    def apply_selected(x):
        out = []
        for s in range(2):
            a, b, c = parts3(x[s])
            stacked = jnp.concatenate([a, b, c, jnp.zeros_like(a)], axis=0).astype(bf16)
            y = nt_dot(stacked, tsel[s])[:, :NT]
            out.append(masks[s] * (y[0:2] + y[2:4] + y[4:6]))
        return out

    locals_[0].wait()
    select(ninv_v)
    direction = apply_selected(start)

    locals_[1].wait()
    d4 = jnp.concatenate(direction, axis=0)
    da, db, dc = parts3(d4)
    d128 = jnp.concatenate([da] * 8 + [db] * 8 + [dc] * 8 + [jnp.zeros_like(da)] * 8, axis=0).astype(bf16)
    lane = lax.broadcasted_iota(jnp.int32, (NS, 128), 1)
    hat = jnp.zeros((NS, 128), f32)
    for part, table in enumerate(parts2(dft_v[...])):
        full = nt_dot(table, d128)
        picked = jnp.zeros((NS, 128), f32)
        for xf in range(8):
            picked += jnp.where((lane % 32) // 4 == xf, full[xf * NS : (xf + 1) * NS], 0.0)
        hat += picked + pltpu.roll(picked, 96, 1)
        if part == 0:
            hat += pltpu.roll(picked, 64, 1)
    hat = jnp.where(lane < 32, hat, 0.0)
    hsend[...] = hat.reshape(NS, 1, 128)

    @pl.loop(1, NS)
    def _(k):
        peer = lax.rem(me + k, NS)

        @pl.when(is_owner(peer))
        def _():
            row_copy(hsend, hrecv, hss, hrs, peer).start()

    pl.loop(FIRST, NS)(start_k)
    hrecv[me] = hsend[me]

    locals_[2].wait()
    select(ncov_v)
    cov = apply_selected(direction)
    inner = sum(jnp.sum(start[s] * direction[s], axis=1, keepdims=True) for s in range(2))
    curve = sum(jnp.sum(cov[s] * direction[s], axis=1, keepdims=True) for s in range(2))
    for copy in locals_[3:]:
        copy.wait()

    lane1 = lax.broadcasted_iota(jnp.int32, (1, 128), 1)
    known = jnp.zeros((1, 128), f32)
    for at, value in ((34, inner[0:1]), (35, inner[1:2]), (36, curve[0:1]), (37, curve[1:2])):
        known += jnp.where(lane1 == at, value, 0.0)

    @pl.when(mine)
    def _():
        @pl.loop(1, NS)
        def _(k):
            peer = lax.rem(me + k, NS)
            row_arrived(hsend, hrecv, hrs, peer).wait()

        rows = hrecv[...]
        twice = rows + pltpu.roll(rows.reshape(NS, 128), 32, 1).reshape(NS, 1, 128)
        z = (jnp.broadcast_to(twice, (NS, 16, 128)) * mask16[...][None]).reshape(NS * 16, 128).astype(bf16)
        h = nt_dot(g[...].astype(bf16), z).astype(bf16)

        @pl.loop(0, NS)
        def _(k):
            k_arrived(lax.rem(me + k, NS)).wait()

        adjoint = jnp.dot(h, kk[...], preferred_element_type=f32).astype(bf16)
        weighted = jnp.dot(adjoint, prior_v[...], preferred_element_type=f32).astype(bf16)
        spread = nt_dot(weighted, prior_v[...]).astype(bf16)
        spread = jnp.dot(gt[...].astype(bf16), spread, preferred_element_type=f32).astype(bf16)
        cross = nt_dot(kk[...], spread)
        folded = (cross.reshape(NS, 16, 128) * mask16[...][None]).sum(axis=1)
        folded = folded + pltpu.roll(folded, 96, 1)
        folded = jnp.where(lane < 32, folded, 0.0)
        bins = FB * my_chunk + (lane % 16) // 4
        weight = jnp.where((bins == 0) | (bins == NT // 2), 1.0, 2.0) / NT
        terms = folded * rows.reshape(NS, 128) * weight
        for r in range(2):
            value = jnp.sum(jnp.where(lane % 2 == r, terms, 0.0), keepdims=True)
            folded = folded + jnp.where(lane == 32 + r, value, 0.0)
        vsend[...] = (folded + known).reshape(NS, 1, 128)

    @pl.when(jnp.logical_not(mine))
    def _():
        vsend[...] = jnp.broadcast_to(known[None], (NS, 1, 128))

    @pl.loop(1, NS)
    def _(k):
        row_copy(vsend, vrecv, vss, vrs, lax.rem(me + k, NS)).start()

    vrecv[me] = vsend[me]

    @pl.loop(1, NS)
    def _(k):
        row_arrived(vsend, vrecv, vrs, lax.rem(me + k, NS)).wait()

    got = vrecv[...].reshape(NS, 128)
    total = jnp.sum(got, axis=0, keepdims=True)
    got = jnp.where(lane < 32, got, 0.0)
    packed = got[0:16]
    for q in range(1, 4):
        packed += pltpu.roll(got[16 * q : 16 * q + 16], 32 * q, 1)
    row16 = lax.broadcasted_iota(jnp.int32, (16, 128), 0)
    lane16 = lax.broadcasted_iota(jnp.int32, (16, 128), 1)
    spare = jnp.broadcast_to(pltpu.roll(jnp.where((lane1 == 32) | (lane1 == 33), total, 0.0), 64, 1), (16, 128))
    packed = jnp.where((row16 == 15) & (lane16 >= 96), spare, packed)
    psend[...] = packed
    precv[mp] = packed

    def p_copy(peer):
        return pltpu.make_async_remote_copy(
            src_ref=psend,
            dst_ref=precv.at[mp],
            send_sem=pss.at[peer],
            recv_sem=prs.at[mp],
            device_id={"pts": peer},
            device_id_type=MESH,
        )

    def p_arrived(peer):
        return pltpu.make_async_copy(psend, precv.at[peer], prs.at[peer])

    @pl.loop(1, NP)
    def _(k):
        p_copy(lax.rem(mp + k, NP)).start()

    @pl.loop(1, NP)
    def _(k):
        p_arrived(lax.rem(mp + k, NP)).wait()

    forward = jnp.sum(precv[...], axis=0)

    def at_lane(x, n):
        return jnp.sum(jnp.where(lax.broadcasted_iota(jnp.int32, x.shape, 1) == n, x, 0.0), axis=1, keepdims=True)

    last = forward[15:16]
    step = [at_lane(total, 34 + r) / (at_lane(last, 96 + r) + at_lane(total, 36 + r)) for r in range(2)]
    fa = forward.astype(bf16)
    fb = (forward - fa.astype(f32)).astype(bf16)
    spread_out = []
    for part in (fa, fb):
        tiled = lax.dot_general(part, rep[...].astype(bf16), (((0,), (0,)), ((), ())), preferred_element_type=f32)
        tiled = (tiled * pick[...]).astype(bf16)
        spread_out.append(jnp.dot(fold[...].astype(bf16), tiled, preferred_element_type=f32)[0:4])
    both = jnp.concatenate(spread_out, axis=0).astype(bf16)
    hi, lo = (jnp.dot(both, table, preferred_element_type=f32) for table in parts2(idft_v[...]))
    signal = hi[0:4] + hi[4:8] + lo[0:4]
    row2 = lax.broadcasted_iota(jnp.int32, (2, NT), 0)
    size = jnp.where(row2 == 0, step[0], step[1])
    for s in range(2):
        image = cov[s] + masks[s] * signal[2 * s : 2 * s + 2]
        sol[s] = size * direction[s]
        res[s] = start[s] - size * image

    @pl.loop(1, NS)
    def _(k):
        peer = lax.rem(me + k, NS)

        @pl.when(is_owner(peer))
        def _():
            k_copy(peer).wait_send()
            row_copy(hsend, hrecv, hss, hrs, peer).wait_send()

        row_copy(vsend, vrecv, vss, vrs, peer).wait_send()

    @pl.loop(1, NP)
    def _(k):
        p_copy(lax.rem(mp + k, NP)).wait_send()


def shards(observed, spectra, prior_factor, noise_cov, noise_inv, sensor_block, window_len):
    c = tables()
    kx = jnp.pad(spectra, ((0, 0), (0, NC * FB - F), (0, 0), (0, 0)))
    kx = kx.reshape(2, NC, FB, 2, PD).transpose(1, 0, 2, 3, 4).reshape(NC, 16, PD)
    vmem, smem, any_ = (pl.BlockSpec(memory_space=m) for m in (pltpu.VMEM, pltpu.SMEM, pl.ANY))
    dma = pltpu.SemaphoreType.DMA
    out = jax.ShapeDtypeStruct((2, 2, NT), f32)
    return pl.pallas_call(
        kernel,
        out_shape=(out, out),
        in_specs=[smem, smem, vmem] + [any_] * 6 + [vmem] * 6,
        out_specs=(vmem, vmem),
        scratch_shapes=[
            pltpu.VMEM((NS * 16, PD), bf16),
            pltpu.VMEM((PD, PD), bf16),
            pltpu.VMEM((TP, NB, NT), bf16),
            pltpu.VMEM((TP, NB, NT), bf16),
            pltpu.VMEM((512, NT), f32),
            pltpu.VMEM((512, NT), f32),
            pltpu.VMEM((2, TP, NT), bf16),
            pltpu.VMEM((NS, 1, 128), f32),
            pltpu.VMEM((NS, 1, 128), f32),
            pltpu.VMEM((NS, 1, 128), f32),
            pltpu.VMEM((NS, 1, 128), f32),
            pltpu.VMEM((16, 128), f32),
            pltpu.VMEM((NP, 16, 128), f32),
            pltpu.VMEM((8, 128), f32),
            dma((5,)),
            dma((NS,)), dma((NS,)), dma((NS,)), dma((NS,)), dma((NS,)), dma((NS,)),
            dma((NP,)), dma((NP,)),
        ],
        compiler_params=pltpu.CompilerParams(
            collective_id=0, has_side_effects=True, vmem_limit_bytes=48 << 20
        ),
        cost_estimate=pl.CostEstimate(flops=10**10, bytes_accessed=10**7, transcendentals=0),
    )(
        window_len, sensor_block, observed, kx, prior_factor,
        noise_inv.transpose(1, 0, 2), noise_cov.transpose(1, 0, 2),
        c["fwd"], c["inv"], c["gt"], c["g"], c["mask"], c["rep"], c["pick"], c["fold"],
    )


def solution(mesh):
    placed = (
        P("sens", None, None),
        P(None, None, "sens", "pts"),
        P("pts", None),
        P(),
        P(),
        P("sens"),
        P("sens"),
    )
    return jax.shard_map(
        shards,
        mesh=mesh,
        in_specs=placed,
        out_specs=(P("sens", None, None), P("sens", None, None)),
        check_vma=False,
    )
```

time: 661 us -> 117 us (0.18)
  blocking collectives: 499 us -> 0 us
  Pallas kernels: 0 us -> 101 us
  waiting for transfers between devices: 86.5 us -> 0 us
  matrix products: 26.3 us -> 0 us
  local copies, waits for them, and re-layouts: 28.4 us -> 14 us
  between operations: 14.9 us -> 0.73 us
    unnamed x1 -> x0, blocking collectives: 327 us -> none
    psum x2 -> x0, blocking collectives: 172 us -> none  [the longest x1 145 us: shards(): inner_total = lax.psum(inner_local, 'sens')]
    pallas_call x0 -> x1, Pallas kernels: none -> 101 us  [shards(): pl.pallas_call(kernel, out_shape=(out, out), in_specs=[smem, smem, vmem]...]
    all_gather x1 -> x0, waiting for transfers between devices: 86.5 us -> none  [shards(): adjoint = lax.all_gather(share_adj, 'sens', axis=3, tiled=True)]
    dot_general x15 -> x0, matrix products: 26.3 us -> none  [the longest x1 4.83 us: shards(): jnp.einsum('xfrq,pq->xfrp', weighted.astype(jnp.bfloat16), prior_factor,...]
    gather x2 -> x0, local copies, waits for them, and re-layouts: 15.1 us -> none  [apply_table(): tables = matrix_set[sensor_block].astype(jnp.float32)]
    another operation x5 -> x0, local copies, waits for them, and re-layouts: 7.02 us -> none  [the longest x1 6.73 us: shards(): partial_adj = jnp.stack([part_re, part_im])]
  transfers between devices with their start and end apart: 1 -> 0, of which waited for: 1 -> 0; matrix products, arithmetic and copies ran while one was open for 1% -> 0% of each run, Pallas kernels for 0% -> 0%
where the time goes in v1:
time: 117 us; the launch traced here: 116 us
  Pallas kernels  101 us (86%)
  local copies, waits for them, and re-layouts  14 us (12%)
    pallas_call x1, Pallas kernels, shards(): pl.pallas_call(kernel, out_shape=(out, out), in_specs=[smem, smem, vmem]...  101 us
    unnamed x26, local copies, waits for them, and re-layouts  6.38 us
    reshape x2, local copies, waits for them, and re-layouts, shards(): kx.reshape(2, NC, FB, 2, PD).transpose(1, 0, 2, 3, 4).reshape(NC, 16, PD)  5.31 us

profile of v1, /device:TPU:1, one launch (start us, length us, event | category | flops | bytes accessed | tf_op | source)
XLA Modules:
  0.0 116.2 jit_solution(16822714648129495695)
XLA Ops:
  0.6 2.3 %pad.4 = bf16[2,212,2,768]{3,2,1,0:T(2,128)(2,1)S(1)} pad(bf16[2,211,2,768]{3,2,1,0:T(2,128)(2,1)} %param.16, bf16[]{:T(256)} %constant.18.clone.1), padding=0_0x0_1x0_0x0_0 | pad | bytes 2598914 | tf_op jit(solution)/shard_map/jit(_pad)/pad | solution.py:363
  3.0 2.0 %copy.19 = bf16[2,53,4,2,768]{4,3,2,0,1:T(2,128)(2,1)} copy(bf16[2,53,4,2,768]{4,3,2,1,0:T(2,128)(2,1)S(1)} %bitcast.6) | data formatting | bytes 2605056 | tf_op jit(solution)/shard_map/reshape | solution.py:364
  4.9 0.0 copy-start
  4.9 0.0 copy-start.1
  4.9 0.0 copy-start.2
  4.9 0.0 copy-start.3
  4.9 0.0 copy-start.4
  5.0 0.0 copy-start.9
  5.0 3.3 %reshape.11.kx = bf16[53,16,768]{2,1,0:T(8,128)(2,1)S(1)} reshape(bf16[53,2,4,2,768]{4,3,2,1,0:T(2,128)(2,1)} %bitcast.7) | data formatting | bytes 2605056 | tf_op jit(solution)/shard_map/reshape | solution.py:364
  8.3 0.0 copy-done
  8.3 0.0 copy-done.1
  8.3 0.0 copy-done.2
  8.3 0.0 copy-done.3
  8.3 0.0 copy-done.4
  8.4 0.0 copy-done.9
  8.4 0.0 copy-start.5
  8.4 1.2 %copy-done.5 = f32[512,420]{1,0:T(8,128)S(1)} copy-done((f32[512,420]{1,0:T(8,128)S(1)}, f32[512,420]{1,0:T(8,128)}, u32[]{:S(2)}) %copy-start.5) | copy-done | bytes 860184
  9.6 0.0 copy-start.6
  9.6 0.9 copy-done.6
  10.5 0.0 copy-start.7
  10.6 0.8 copy-done.7
  11.4 0.0 copy-start.8
  11.4 0.8 copy-done.8
  12.1 0.0 copy-start.10
  12.1 0.7 copy-done.10
  12.8 0.0 copy-start.11
  12.8 0.7 copy-done.11
  13.5 101.4 %shard_map.158 = (f32[2,2,420]{2,1,0:T(2,128)S(1)}, f32[2,2,420]{2,1,0:T(2,128)S(1)}) custom-call(s32[2]{0:T(128)S(1)} %copy-done.2, s32[2]{0:T(128)S(1)} %copy-done.3, f32[2,2,420]{2,1,0:T(2,128)S(1)} %copy-done.1, bf16[53,16,768]{2,1,0:T(8,128)(2,1)S(1)} %reshape.11.kx, bf16[768,768]{1,0:T(8,128)(2,1)S(1)} %copy-done, bf16[420,4,420]{2,1,0:T(4,128)(2,1)} %bitcast.8, ...), custom_call_target="tpu_custom_call" | custom-call | flops 10000000000 | bytes 10000000 | tf_op jit(solution)/shard_map/pallas_call | solution.py:368
  115.0 0.6 copy.22
  115.6 0.6 copy.23
Async XLA Ops:
  4.9 3.4 %copy-start = (bf16[768,768]{1,0:T(8,128)(2,1)S(1)}, bf16[768,768]{1,0:T(8,128)(2,1)}, u32[]{:S(2)}) copy-start(bf16[768,768]{1,0:T(8,128)(2,1)} %prior.1) | copy-start | bytes 3538948
  4.9 3.4 %copy-start.1 = (f32[2,2,420]{2,1,0:T(2,128)S(1)}, f32[2,2,420]{2,1,0:T(2,128)}, u32[]{:S(2)}) copy-start(f32[2,2,420]{2,1,0:T(2,128)} %obs.1) | copy-start | bytes 20164
  4.9 3.4 %copy-start.2 = (s32[2]{0:T(128)S(1)}, s32[2]{0:T(128)}, u32[]{:S(2)}) copy-start(s32[2]{0:T(128)} %wl.1) | copy-start | bytes 28
  4.9 3.4 %copy-start.3 = (s32[2]{0:T(128)S(1)}, s32[2]{0:T(128)}, u32[]{:S(2)}) copy-start(s32[2]{0:T(128)} %sb.1) | copy-start | bytes 28
  4.9 3.4 %copy-start.4 = (f32[512,420]{1,0:T(8,128)S(1)}, f32[512,420]{1,0:T(8,128)}, u32[]{:S(2)}) copy-start(f32[512,420]{1,0:T(8,128)} %constant.20.clone.idft) | copy-start | bytes 2580484
  5.0 3.4 %copy-start.9 = (f32[16,128]{1,0:T(8,128)S(1)}, f32[16,128]{1,0:T(8,128)}, u32[]{:S(2)}) copy-start(f32[16,128]{1,0:T(8,128)} %constant.23.clone.mask16) | copy-start | bytes 24580
  8.4 1.2 %copy-start.5 = (f32[512,420]{1,0:T(8,128)S(1)}, f32[512,420]{1,0:T(8,128)}, u32[]{:S(2)}) copy-start(f32[512,420]{1,0:T(8,128)} %constant.19.clone.dft) | copy-start | bytes 2580484
  9.6 0.9 copy-start.6
  10.5 0.8 copy-start.7
  11.4 0.8 copy-start.8
  12.1 0.7 copy-start.10
  12.8 0.7 copy-start.11

commit v2 on v1

v2 whole, which is shorter than its diff:
```python
import functools
import math

import jax
import jax.numpy as jnp
import numpy as np
from jax import lax
from jax.experimental import pallas as pl
from jax.experimental.pallas import tpu as pltpu
from jax.sharding import PartitionSpec as P

MESH = pl.DeviceIdType.MESH
NT, F, PD, NB = 420, 211, 768, 4
NS, NP = 64, 16
FB = 4
NC = -(-F // FB)
TP = 432
FIRST = 40
f32, bf16 = jnp.float32, jnp.bfloat16


def chunk_of(dev):
    return (dev * NC + NS - 1) // NS


def first_bin(c):
    return jnp.minimum(FB * c, F - FB)


def is_owner(dev):
    return chunk_of(dev + 1) != chunk_of(dev)


@functools.cache
def tables():
    t = np.arange(NT)
    fwd = np.zeros((2, FB, NS, NT))
    inv = np.zeros((NS, 2, FB, NT))
    for dev in range(NS):
        c = -(-dev * NC // NS)
        if (c * NS) // NC != dev or c >= NC:
            continue
        for f in range(FB):
            bin_ = min(FB * c, F - FB) + f
            if bin_ < FB * c:
                continue
            phase = (t * bin_) % NT
            cosine = np.cos(2 * math.pi * phase / NT)
            sine = np.where(phase % (NT // 2) == 0, 0.0, np.sin(2 * math.pi * phase / NT))
            weight = (1.0 if bin_ in (0, NT // 2) else 2.0) / NT
            fwd[0, f, dev], fwd[1, f, dev] = cosine, -sine
            inv[dev, 0, f], inv[dev, 1, f] = cosine * weight, -sine * weight
    fwd = fwd.reshape(2 * FB * NS, NT)
    inv = inv.reshape(4, 16, 8, NT).transpose(0, 2, 1, 3).reshape(512, NT)
    gt = np.zeros((128, 16))
    mask = np.zeros((16, 128))
    for xk in range(2):
        for x in range(2):
            for f in range(FB):
                for s in range(2):
                    mask[xk * 8 + f * 2 + s, xk * 32 + x * 16 + f * 4 + s * 2 :][:2] = 1
                    for r in range(2):
                        m = xk * 32 + x * 16 + f * 4 + s * 2 + r
                        j = f * 4 + (x if xk == 0 else 1 - x) * 2 + r
                        gt[m, j] = 1 if xk == 0 or x == 1 else -1
    rep = np.tile(np.eye(16), (1, 32))
    pick = np.zeros((128, 512))
    for row in range(128):
        pick[row, (row // 4) * 16 : (row // 4) * 16 + 16] = 1
    fold = np.zeros((8, 128))
    for row in range(128):
        fold[row % 4, row] = 1
    small = np.zeros((312, 512))
    small[0:128] = pick
    small[128:144] = rep
    small[144:160, :128] = gt.T
    small[160:176, :128] = mask
    small[176:304, :16] = gt
    small[304:312, :128] = fold
    return [a.astype(np.float32) for a in (fwd, inv, small)]


def parts3(x):
    a = x.astype(bf16).astype(f32)
    b = (x - a).astype(bf16).astype(f32)
    return a, b, x - a - b


def parts2(x):
    a = x.astype(bf16)
    return a, (x - a.astype(f32)).astype(bf16)


def nt_dot(a, b):
    return lax.dot_general(a, b, (((1,), (1,)), ((), ())), preferred_element_type=f32)


def kernel(
    wl, sb, obs, kx, prior, ninv, ncov, dft, idft, small,
    sol, res,
    raw, kk, prior_v, ninv_v, ncov_v, dft_v, idft_v, tsel, hsend, hrecv, vsend, vrecv, psend, precv, small_v,
    lsem, ksend, krecv, hss, hrs, vss, vrs, pss, prs,
):
    me, mp = lax.axis_index("sens"), lax.axis_index("pts")
    mine = is_owner(me)
    my_chunk = chunk_of(me)

    locals_ = [
        pltpu.make_async_copy(ninv, ninv_v.at[pl.ds(0, NT)], lsem.at[0]),
        pltpu.make_async_copy(dft, dft_v, lsem.at[1]),
        pltpu.make_async_copy(ncov, ncov_v.at[pl.ds(0, NT)], lsem.at[2]),
        pltpu.make_async_copy(prior, prior_v, lsem.at[3]),
        pltpu.make_async_copy(small, small_v, lsem.at[4]),
        pltpu.make_async_copy(idft, idft_v, lsem.at[5]),
    ]
    for copy in locals_:
        copy.start()

    scope = jax.named_scope
    barrier = pltpu.get_barrier_semaphore()

    @pl.loop(1, NS)
    def _(k):
        pl.semaphore_signal(barrier, inc=1, device_id={"sens": lax.rem(me + k, NS)}, device_id_type=MESH)

    @pl.loop(1, NP)
    def _(k):
        pl.semaphore_signal(barrier, inc=1, device_id={"pts": lax.rem(mp + k, NP)}, device_id_type=MESH)

    with scope("entry_barrier"):
        pl.semaphore_wait(barrier, NS + NP - 2)

    at_z, at_x, at_core = me // 16, (me // 2) % 8, me % 2

    def partner(k):
        return ((at_z + k % 4) % 4) * 16 + ((at_x + (k // 4) % 8) % 8) * 2 + (at_core + k // 32) % 2

    def k_copy(peer):
        return pltpu.make_async_remote_copy(
            src_ref=kx.at[:, pl.ds(first_bin(chunk_of(peer)), FB)],
            dst_ref=raw.at[me],
            send_sem=ksend.at[peer],
            recv_sem=krecv.at[me],
            device_id={"sens": peer},
            device_id_type=MESH,
        )

    def k_arrived(peer):
        return pltpu.make_async_copy(kx.at[:, pl.ds(0, FB)], raw.at[peer], krecv.at[peer])

    def row_copy(src, dst, ss, rs, peer):
        return pltpu.make_async_remote_copy(
            src_ref=src.at[peer],
            dst_ref=dst.at[me],
            send_sem=ss.at[peer],
            recv_sem=rs.at[me],
            device_id={"sens": peer},
            device_id_type=MESH,
        )

    def row_arrived(src, dst, rs, peer):
        return pltpu.make_async_copy(src.at[peer], dst.at[peer], rs.at[peer])

    def start_k(k):
        peer = partner(k)

        @pl.when(is_owner(peer))
        def _():
            k_copy(peer).start()

    own = pltpu.make_async_copy(kx.at[:, pl.ds(first_bin(my_chunk), FB)], raw.at[me], krecv.at[me])

    @pl.when(mine)
    def _():
        own.start()

    with scope("send_spectra_first"):
        pl.loop(1, FIRST)(start_k)

    time = lax.broadcasted_iota(jnp.int32, (2, NT), 1)
    masks = [(time < wl[s]).astype(f32) for s in range(2)]
    start = [obs[s] * masks[s] for s in range(2)]

    def select(table_v):
        @pl.loop(0, TP // 16)
        def _(i):
            rows = pl.ds(pl.multiple_of(i * 16, 16), 16)
            block = table_v[rows].astype(f32)
            which = lax.broadcasted_iota(jnp.int32, block.shape, 1)
            for s in range(2):
                tsel[s, rows, :] = jnp.where(which == sb[s], block, 0.0).sum(axis=1).astype(bf16)

    def apply_selected(x):
        out = []
        for s in range(2):
            a, b, c = parts3(x[s])
            stacked = jnp.concatenate([a, b, c, jnp.zeros_like(a)], axis=0).astype(bf16)
            y = nt_dot(stacked, tsel[s])[:, :NT]
            out.append(masks[s] * (y[0:2] + y[2:4] + y[4:6]))
        return out

    with scope("direction"):
        locals_[0].wait()
        select(ninv_v)
        direction = apply_selected(start)

    with scope("spectrum"):
        locals_[1].wait()
        d4 = jnp.concatenate(direction, axis=0)
        da, db, dc = parts3(d4)
        d128 = jnp.concatenate([da] * 8 + [db] * 8 + [dc] * 8 + [jnp.zeros_like(da)] * 8, axis=0).astype(bf16)
        lane = lax.broadcasted_iota(jnp.int32, (NS, 128), 1)
        hat = jnp.zeros((NS, 128), f32)
        for part, table in enumerate(parts2(dft_v[...])):
            full = nt_dot(table, d128)
            picked = jnp.zeros((NS, 128), f32)
            for xf in range(8):
                picked += jnp.where((lane % 32) // 4 == xf, full[xf * NS : (xf + 1) * NS], 0.0)
            hat += picked + pltpu.roll(picked, 96, 1)
            if part == 0:
                hat += pltpu.roll(picked, 64, 1)
        hat = jnp.where(lane < 32, hat, 0.0)
        hsend[...] = hat.reshape(NS, 1, 128)

    with scope("send_spectrum_rows"):
        @pl.loop(1, NS)
        def _(k):
            peer = partner(k)

            @pl.when(is_owner(peer))
            def _():
                row_copy(hsend, hrecv, hss, hrs, peer).start()

    with scope("send_spectra_rest"):
        pl.loop(FIRST, NS)(start_k)
    hrecv[me] = hsend[me]

    with scope("covariance"):
        locals_[2].wait()
        select(ncov_v)
        cov = apply_selected(direction)
        inner = sum(jnp.sum(start[s] * direction[s], axis=1, keepdims=True) for s in range(2))
        curve = sum(jnp.sum(cov[s] * direction[s], axis=1, keepdims=True) for s in range(2))
        for copy in locals_[3:]:
            copy.wait()

        lane1 = lax.broadcasted_iota(jnp.int32, (1, 128), 1)
        known = jnp.zeros((1, 128), f32)
        for at, value in ((34, inner[0:1]), (35, inner[1:2]), (36, curve[0:1]), (37, curve[1:2])):
            known += jnp.where(lane1 == at, value, 0.0)

    with scope("bins"):
        @pl.when(mine)
        def _():
            @pl.loop(1, NS)
            def _(k):
                peer = partner(k)
                row_arrived(hsend, hrecv, hrs, peer).wait()

            rows = hrecv[...]
            twice = rows + pltpu.roll(rows.reshape(NS, 128), 32, 1).reshape(NS, 1, 128)
            z = (jnp.broadcast_to(twice, (NS, 16, 128)) * small_v[160:176, 0:128][None]).reshape(NS * 16, 128).astype(bf16)
            h = nt_dot(small_v[144:160, 0:128].astype(bf16), z).astype(bf16)

            with scope("wait_spectra"):

                @pl.loop(0, NS)
                def _(k):
                    peer = partner(k)
                    k_arrived(peer).wait()
                    kk[pl.ds(pl.multiple_of(peer * 16, 16), 16), :] = raw[peer].reshape(16, PD)

            adjoint = jnp.dot(h, kk[...], preferred_element_type=f32).astype(bf16)
            weighted = jnp.dot(adjoint, prior_v[...], preferred_element_type=f32).astype(bf16)
            spread = nt_dot(weighted, prior_v[...]).astype(bf16)
            spread = jnp.dot(small_v[176:304, 0:16].astype(bf16), spread, preferred_element_type=f32).astype(bf16)
            cross = nt_dot(kk[...], spread)
            folded = (cross.reshape(NS, 16, 128) * small_v[160:176, 0:128][None]).sum(axis=1)
            folded = folded + pltpu.roll(folded, 96, 1)
            folded = jnp.where(lane < 32, folded, 0.0)
            bins = first_bin(my_chunk) + (lane % 16) // 4
            weight = jnp.where((bins == 0) | (bins == NT // 2), 1.0, 2.0) / NT
            terms = folded * rows.reshape(NS, 128) * weight
            for r in range(2):
                value = jnp.sum(jnp.where(lane % 2 == r, terms, 0.0), keepdims=True)
                folded = folded + jnp.where(lane == 32 + r, value, 0.0)
            vsend[...] = (folded + known).reshape(NS, 1, 128)

    @pl.when(jnp.logical_not(mine))
    def _():
        vsend[...] = jnp.broadcast_to(known[None], (NS, 1, 128))

    with scope("send_forward_rows"):
        @pl.loop(1, NS)
        def _(k):
            row_copy(vsend, vrecv, vss, vrs, partner(k)).start()

    vrecv[me] = vsend[me]

    with scope("wait_spectra_sent"):

        @pl.loop(1, NS)
        def _(k):
            peer = partner(k)

            @pl.when(is_owner(peer))
            def _():
                k_copy(peer).wait_send()
                row_copy(hsend, hrecv, hss, hrs, peer).wait_send()

    with scope("wait_forward_rows"):

        @pl.loop(1, NS)
        def _(k):
            row_arrived(vsend, vrecv, vrs, partner(k)).wait()

    got = vrecv[...].reshape(NS, 128)
    total = jnp.sum(got, axis=0, keepdims=True)
    got = jnp.where(lane < 32, got, 0.0)
    packed = got[0:16]
    for q in range(1, 4):
        packed += pltpu.roll(got[16 * q : 16 * q + 16], 32 * q, 1)
    row16 = lax.broadcasted_iota(jnp.int32, (16, 128), 0)
    lane16 = lax.broadcasted_iota(jnp.int32, (16, 128), 1)
    spare = jnp.broadcast_to(pltpu.roll(jnp.where((lane1 == 32) | (lane1 == 33), total, 0.0), 64, 1), (16, 128))
    packed = jnp.where((row16 == 15) & (lane16 >= 96), spare, packed)
    psend[...] = packed
    precv[mp] = packed

    def p_copy(peer):
        return pltpu.make_async_remote_copy(
            src_ref=psend,
            dst_ref=precv.at[mp],
            send_sem=pss.at[peer],
            recv_sem=prs.at[mp],
            device_id={"pts": peer},
            device_id_type=MESH,
        )

    def p_arrived(peer):
        return pltpu.make_async_copy(psend, precv.at[peer], prs.at[peer])

    with scope("send_over_pts"):

        @pl.loop(1, NP)
        def _(k):
            p_copy(lax.rem(mp + k, NP)).start()

    with scope("wait_forward_sent"):

        @pl.loop(1, NS)
        def _(k):
            row_copy(vsend, vrecv, vss, vrs, partner(k)).wait_send()

    with scope("wait_over_pts"):

        @pl.loop(1, NP)
        def _(k):
            p_arrived(lax.rem(mp + k, NP)).wait()

    forward = jnp.sum(precv[...], axis=0)

    def at_lane(x, n):
        return jnp.sum(jnp.where(lax.broadcasted_iota(jnp.int32, x.shape, 1) == n, x, 0.0), axis=1, keepdims=True)

    last = forward[15:16]
    step = [at_lane(total, 34 + r) / (at_lane(last, 96 + r) + at_lane(total, 36 + r)) for r in range(2)]
    fa = forward.astype(bf16)
    fb = (forward - fa.astype(f32)).astype(bf16)
    spread_out = []
    for part in (fa, fb):
        tiled = lax.dot_general(part, small_v[128:144].astype(bf16), (((0,), (0,)), ((), ())), preferred_element_type=f32)
        tiled = (tiled * small_v[0:128]).astype(bf16)
        spread_out.append(jnp.dot(small_v[304:312, 0:128].astype(bf16), tiled, preferred_element_type=f32)[0:4])
    both = jnp.concatenate(spread_out, axis=0).astype(bf16)
    hi, lo = (jnp.dot(both, table, preferred_element_type=f32) for table in parts2(idft_v[...]))
    signal = hi[0:4] + hi[4:8] + lo[0:4]
    row2 = lax.broadcasted_iota(jnp.int32, (2, NT), 0)
    size = jnp.where(row2 == 0, step[0], step[1])
    for s in range(2):
        image = cov[s] + masks[s] * signal[2 * s : 2 * s + 2]
        sol[s] = size * direction[s]
        res[s] = start[s] - size * image

    @pl.loop(1, NP)
    def _(k):
        p_copy(lax.rem(mp + k, NP)).wait_send()


def shards(observed, spectra, prior_factor, noise_cov, noise_inv, sensor_block, window_len):
    vmem, smem, any_ = (pl.BlockSpec(memory_space=m) for m in (pltpu.VMEM, pltpu.SMEM, pl.ANY))
    dma = pltpu.SemaphoreType.DMA
    out = jax.ShapeDtypeStruct((2, 2, NT), f32)
    return pl.pallas_call(
        kernel,
        out_shape=(out, out),
        in_specs=[smem, smem, vmem] + [any_] * 7,
        out_specs=(vmem, vmem),
        scratch_shapes=[
            pltpu.VMEM((NS, 2, FB, 2, PD), bf16),
            pltpu.VMEM((NS * 16, PD), bf16),
            pltpu.VMEM((PD, PD), bf16),
            pltpu.VMEM((TP, NB, NT), bf16),
            pltpu.VMEM((TP, NB, NT), bf16),
            pltpu.VMEM((512, NT), f32),
            pltpu.VMEM((512, NT), f32),
            pltpu.VMEM((2, TP, NT), bf16),
            pltpu.VMEM((NS, 1, 128), f32),
            pltpu.VMEM((NS, 1, 128), f32),
            pltpu.VMEM((NS, 1, 128), f32),
            pltpu.VMEM((NS, 1, 128), f32),
            pltpu.VMEM((16, 128), f32),
            pltpu.VMEM((NP, 16, 128), f32),
            pltpu.VMEM((312, 512), f32),
            dma((6,)),
            dma((NS,)), dma((NS,)), dma((NS,)), dma((NS,)), dma((NS,)), dma((NS,)),
            dma((NP,)), dma((NP,)),
        ],
        compiler_params=pltpu.CompilerParams(
            collective_id=0, has_side_effects=True, vmem_limit_bytes=60 << 20
        ),
        cost_estimate=pl.CostEstimate(flops=10**10, bytes_accessed=10**7, transcendentals=0),
    )(
        window_len, sensor_block, observed, spectra, prior_factor,
        noise_inv.transpose(1, 0, 2), noise_cov.transpose(1, 0, 2),
        *tables(),
    )


def solution(mesh):
    placed = (
        P("sens", None, None),
        P(None, None, "sens", "pts"),
        P("pts", None),
        P(),
        P(),
        P("sens"),
        P("sens"),
    )
    return jax.shard_map(
        shards,
        mesh=mesh,
        in_specs=placed,
        out_specs=(P("sens", None, None), P("sens", None, None)),
        check_vma=False,
    )
```

time: 117 us -> 93.2 us (0.80)
  Pallas kernels: 101 us -> 88.9 us
  local copies, waits for them, and re-layouts: 14 us -> 2.59 us
    pallas_call x1, Pallas kernels: 101 us -> 88.9 us  [shards(): pl.pallas_call(kernel, out_shape=(out, out), in_specs=[smem, smem, vmem]...]
    reshape x2 -> x0, local copies, waits for them, and re-layouts: 5.31 us -> none  [shards(): kx.reshape(2, NC, FB, 2, PD).transpose(1, 0, 2, 3, 4).reshape(NC, 16, PD)]
    unnamed x26 -> x2, local copies, waits for them, and re-layouts: 6.38 us -> 2.59 us
    pad x1 -> x0, local copies, waits for them, and re-layouts: 2.32 us -> none  [shards(): kx = jnp.pad(spectra, ((0, 0), (0, NC * FB - F), (0, 0), (0, 0)))]
where the time goes in v2:
time: 93.2 us; the launch traced here: 92.2 us
  Pallas kernels  88.9 us (95%)
  local copies, waits for them, and re-layouts  2.59 us (3%)
    pallas_call x1, Pallas kernels, shards(): pl.pallas_call(kernel, out_shape=(out, out), in_specs=[smem, smem, vmem]...  88.9 us
    unnamed x2, local copies, waits for them, and re-layouts  2.59 us

profile of v2, /device:TPU:1, one launch (start us, length us, event | category | flops | bytes accessed | tf_op | source)
XLA Modules:
  0.0 92.2 jit_solution(8479603982296736383)
XLA Ops:
  0.6 88.9 %shard_map.113 = (f32[2,2,420]{2,1,0:T(2,128)}, f32[2,2,420]{2,1,0:T(2,128)}) custom-call(s32[2]{0:T(128)} %wl.1, s32[2]{0:T(128)} %sb.1, f32[2,2,420]{2,1,0:T(2,128)} %obs.1, bf16[2,211,2,768]{3,2,1,0:T(2,128)(2,1)} %kx.1, bf16[768,768]{1,0:T(8,128)(2,1)} %prior.1, bf16[420,4,420]{2,1,0:T(4,128)(2,1)} %bitcast.2, bf16[420,4,420]{2,1,0:T(4,128)(2,1)} %bitcast.3, ...), custom_call_target="tpu_custom_call" | custom-call | flops 10000000000 | bytes 10000000 | tf_op jit(solution)/shard_map/pallas_call | solution.py:394
  89.6 1.3 %copy.14 = f32[2,2,420]{2,1,0:T(2,128)} copy(f32[2,2,420]{2,1,0:T(2,128)} %get-tuple-element.4) | data formatting | bytes 13440
  90.9 1.3 %copy.15 = f32[2,2,420]{2,1,0:T(2,128)} copy(f32[2,2,420]{2,1,0:T(2,128)} %get-tuple-element.5) | data formatting | bytes 13440

commit v3 on v1

v3 whole, which is shorter than its diff:
```python
import functools
import math

import jax
import jax.numpy as jnp
import numpy as np
from jax import lax
from jax.experimental import pallas as pl
from jax.experimental.pallas import tpu as pltpu
from jax.sharding import PartitionSpec as P

MESH = pl.DeviceIdType.MESH
NT, F, PD, NB = 420, 211, 768, 4
NS, NP = 64, 16
FB = 4
NC = -(-F // FB)
TP = 432
f32, bf16 = jnp.float32, jnp.bfloat16


def chunk_of(dev):
    return (dev * NC + NS - 1) // NS


def first_bin(c):
    return jnp.minimum(FB * c, F - FB)


def is_owner(dev):
    return chunk_of(dev + 1) != chunk_of(dev)


@functools.cache
def tables():
    t = np.arange(NT)
    fwd = np.zeros((2, FB, NS, NT))
    inv = np.zeros((NS, 2, FB, NT))
    for dev in range(NS):
        c = -(-dev * NC // NS)
        if (c * NS) // NC != dev or c >= NC:
            continue
        for f in range(FB):
            bin_ = min(FB * c, F - FB) + f
            if bin_ < FB * c:
                continue
            phase = (t * bin_) % NT
            cosine = np.cos(2 * math.pi * phase / NT)
            sine = np.where(phase % (NT // 2) == 0, 0.0, np.sin(2 * math.pi * phase / NT))
            weight = (1.0 if bin_ in (0, NT // 2) else 2.0) / NT
            fwd[0, f, dev], fwd[1, f, dev] = cosine, -sine
            inv[dev, 0, f], inv[dev, 1, f] = cosine * weight, -sine * weight
    fwd = fwd.reshape(2 * FB * NS, NT)
    inv = inv.reshape(4, 16, 8, NT).transpose(0, 2, 1, 3).reshape(512, NT)
    gt = np.zeros((128, 16))
    mask = np.zeros((16, 128))
    for xk in range(2):
        for x in range(2):
            for f in range(FB):
                for s in range(2):
                    mask[xk * 8 + f * 2 + s, xk * 32 + x * 16 + f * 4 + s * 2 :][:2] = 1
                    for r in range(2):
                        m = xk * 32 + x * 16 + f * 4 + s * 2 + r
                        j = f * 4 + (x if xk == 0 else 1 - x) * 2 + r
                        gt[m, j] = 1 if xk == 0 or x == 1 else -1
    rep = np.tile(np.eye(16), (1, 32))
    pick = np.zeros((128, 512))
    for row in range(128):
        pick[row, (row // 4) * 16 : (row // 4) * 16 + 16] = 1
    fold = np.zeros((8, 128))
    for row in range(128):
        fold[row % 4, row] = 1
    small = np.zeros((312, 512))
    small[0:128] = pick
    small[128:144] = rep
    small[144:160, :128] = gt.T
    small[160:176, :128] = mask
    small[176:304, :16] = gt
    small[304:312, :128] = fold
    return [a.astype(np.float32) for a in (fwd, inv, small)]


def parts3(x):
    a = x.astype(bf16).astype(f32)
    b = (x - a).astype(bf16).astype(f32)
    return a, b, x - a - b


def parts2(x):
    a = x.astype(bf16)
    return a, (x - a.astype(f32)).astype(bf16)


def nt_dot(a, b):
    return lax.dot_general(a, b, (((1,), (1,)), ((), ())), preferred_element_type=f32)


def kernel(
    wl_any, sb_any, obs_any, kx, prior, ninv, ncov, dft, idft, small,
    out,
    wl, sb, obs, raw, kk, prior_v, ninv_v, ncov_v, dft_v, idft_v, idft_2, tsel, hsend, hrecv, vsend, vrecv, psend, precv, small_v,
    lsem, krecv, ksend, hss, hrs, vss, vrs, pss, prs,
):
    me, mp = lax.axis_index("sens"), lax.axis_index("pts")
    mine = is_owner(me)
    my_chunk = chunk_of(me)
    at_x, in_z, in_core = (me // 2) % 8, me // 16, me % 2
    at_z = [((in_z + dz) % 4) * 16 for dz in range(4)]
    at_core = [in_core, 1 - in_core]

    def partners(body, low=0, high=4):
        @pl.loop(low, high)
        def _(t):
            for back_x in range(2):
                step = t if back_x == 0 else jnp.where(t == 0, 4, 8 - t)
                x = ((at_x + step) % 8) * 2
                there = jnp.where(t == 0, back_x, 1 - back_x) * 8 + t * 16
                for dz in range(4):
                    for dc in range(2):
                        todo = functools.partial(
                            body,
                            at_z[dz] + x + at_core[dc],
                            t * 16 + back_x * 8 + dz * 2 + dc,
                            there + (-dz % 4) * 2 + dc,
                            t,
                        )
                        if back_x == dz == dc == 0:
                            pl.when(t != 0)(todo)
                        else:
                            todo()

    def others(body):
        for k in range(1, NP):
            body((mp + k) % NP)

    barrier = pltpu.get_barrier_semaphore()
    partners(
        lambda peer, *_: pl.semaphore_signal(barrier, inc=1, device_id={"sens": peer}, device_id_type=MESH)
    )
    others(lambda peer: pl.semaphore_signal(barrier, inc=1, device_id={"pts": peer}, device_id_type=MESH))

    locals_ = [
        pltpu.make_async_copy(wl_any, wl, lsem.at[0]),
        pltpu.make_async_copy(sb_any, sb, lsem.at[1]),
        pltpu.make_async_copy(obs_any, obs, lsem.at[2]),
        pltpu.make_async_copy(ninv, ninv_v.at[pl.ds(0, NT)], lsem.at[3]),
        pltpu.make_async_copy(dft, dft_v, lsem.at[4]),
        pltpu.make_async_copy(ncov, ncov_v.at[pl.ds(0, NT)], lsem.at[5]),
        pltpu.make_async_copy(prior, prior_v, lsem.at[6]),
        pltpu.make_async_copy(small, small_v, lsem.at[7]),
        pltpu.make_async_copy(idft, idft_v, lsem.at[8]),
    ]
    for copy in locals_:
        copy.start()
    own = pltpu.make_async_copy(kx.at[:, pl.ds(first_bin(jnp.minimum(my_chunk, NC - 1)), FB)], raw.at[0], krecv.at[0])

    @pl.when(mine)
    def _():
        own.start()

    pl.semaphore_wait(barrier, NS + NP - 2)

    def remote(src, dst, send, recv, peer):
        return pltpu.make_async_remote_copy(
            src_ref=src, dst_ref=dst, send_sem=send, recv_sem=recv, device_id=peer, device_id_type=MESH
        )

    def finish(like, sem):
        pltpu.make_async_copy(like, like, sem).wait()

    def send_bins(peer, slot, there, t):
        @pl.when(is_owner(peer))
        def _():
            first = first_bin(chunk_of(peer))
            remote(kx.at[:, pl.ds(first, FB)], raw.at[there], ksend, krecv.at[t], {"sens": peer}).start()

    partners(send_bins, 0, 3)

    for copy in locals_[:4]:
        copy.wait()

    time = lax.broadcasted_iota(jnp.int32, (2, NT), 1)
    masks = [(time < wl[s]).astype(f32) for s in range(2)]
    start = [obs[s] * masks[s] for s in range(2)]

    def select(table_v):
        @pl.loop(0, TP // 16)
        def _(i):
            rows = pl.ds(pl.multiple_of(i * 16, 16), 16)
            block = table_v[rows].astype(f32)
            which = lax.broadcasted_iota(jnp.int32, block.shape, 1)
            for s in range(2):
                tsel[s, rows, :] = jnp.where(which == sb[s], block, 0.0).sum(axis=1).astype(bf16)

    def apply_selected(x):
        out = []
        for s in range(2):
            a, b, c = parts3(x[s])
            stacked = jnp.concatenate([a, b, c, jnp.zeros_like(a)], axis=0).astype(bf16)
            y = nt_dot(stacked, tsel[s])[:, :NT]
            out.append(masks[s] * (y[0:2] + y[2:4] + y[4:6]))
        return out

    select(ninv_v)
    direction = apply_selected(start)

    locals_[4].wait()
    d4 = jnp.concatenate(direction, axis=0)
    da, db, dc = parts3(d4)
    d128 = jnp.concatenate([da] * 8 + [db] * 8 + [dc] * 8 + [jnp.zeros_like(da)] * 8, axis=0).astype(bf16)
    lane = lax.broadcasted_iota(jnp.int32, (NS, 128), 1)
    hat = jnp.zeros((NS, 128), f32)
    for part, table in enumerate(parts2(dft_v[...])):
        full = nt_dot(table, d128)
        picked = jnp.zeros((NS, 128), f32)
        for xf in range(8):
            picked += jnp.where((lane % 32) // 4 == xf, full[xf * NS : (xf + 1) * NS], 0.0)
        hat += picked + pltpu.roll(picked, 96, 1)
        if part == 0:
            hat += pltpu.roll(picked, 64, 1)
    hat = jnp.where(lane < 32, hat, 0.0)
    hsend[...] = hat.reshape(NS, 1, 128)

    def send_hat(peer, slot, there, t):
        @pl.when(is_owner(peer))
        def _():
            remote(hsend.at[peer], hrecv.at[there], hss, hrs, {"sens": peer}).start()

    partners(send_hat)
    partners(send_bins, 3, 4)
    hrecv[0] = hsend[me]

    locals_[5].wait()
    select(ncov_v)
    cov = apply_selected(direction)
    inner = sum(jnp.sum(start[s] * direction[s], axis=1, keepdims=True) for s in range(2))
    curve = sum(jnp.sum(cov[s] * direction[s], axis=1, keepdims=True) for s in range(2))
    for copy in locals_[6:]:
        copy.wait()
    idft_2[0], idft_2[1] = parts2(idft_v[...])

    lane1 = lax.broadcasted_iota(jnp.int32, (1, 128), 1)
    known = jnp.zeros((1, 128), f32)
    for at, value in ((34, inner[0:1]), (35, inner[1:2]), (36, curve[0:1]), (37, curve[1:2])):
        known += jnp.where(lane1 == at, value, 0.0)
    mask16 = small_v[160:176, 0:128]

    @pl.when(mine)
    def _():
        finish(hrecv.at[pl.ds(0, NS - 1)], hrs)
        rows = hrecv[...]
        twice = rows + pltpu.roll(rows.reshape(NS, 128), 32, 1).reshape(NS, 1, 128)
        z = (jnp.broadcast_to(twice, (NS, 16, 128)) * mask16[None]).reshape(NS * 16, 128).astype(bf16)
        h = nt_dot(small_v[144:160, 0:128].astype(bf16), z).astype(bf16)

        @pl.loop(0, 4)
        def _(t):
            finish(raw.at[pl.ds(t * 16, 16)], krecv.at[t])

            @pl.loop(0, 16)
            def _(i):
                slot = t * 16 + i
                kk[pl.ds(pl.multiple_of(slot * 16, 16), 16), :] = raw[slot].reshape(16, PD)

        adjoint = jnp.dot(h, kk[...], preferred_element_type=f32).astype(bf16)
        weighted = jnp.dot(adjoint, prior_v[...], preferred_element_type=f32).astype(bf16)
        spread = nt_dot(weighted, prior_v[...]).astype(bf16)
        spread = jnp.dot(small_v[176:304, 0:16].astype(bf16), spread, preferred_element_type=f32).astype(bf16)
        cross = nt_dot(kk[...], spread)
        folded = (cross.reshape(NS, 16, 128) * mask16[None]).sum(axis=1)
        folded = folded + pltpu.roll(folded, 96, 1)
        folded = jnp.where(lane < 32, folded, 0.0)
        bins = first_bin(my_chunk) + (lane % 16) // 4
        weight = jnp.where((bins == 0) | (bins == NT // 2), 1.0, 2.0) / NT
        terms = folded * rows.reshape(NS, 128) * weight
        for r in range(2):
            value = jnp.sum(jnp.where(lane % 2 == r, terms, 0.0), keepdims=True)
            folded = folded + jnp.where(lane == 32 + r, value, 0.0)
        vsend[...] = (folded + known).reshape(NS, 1, 128)

    @pl.when(jnp.logical_not(mine))
    def _():
        vsend[...] = jnp.broadcast_to(known[None], (NS, 1, 128))

    partners(lambda peer, slot, there, t: remote(vsend.at[slot], vrecv.at[me], vss, vrs, {"sens": peer}).start())
    vrecv[me] = vsend[0]

    for is_mine, count in ((mine, NC - 1), (jnp.logical_not(mine), NC)):

        @pl.when(is_mine)
        def _():
            finish(raw.at[pl.ds(0, count)], ksend)
            finish(hsend.at[pl.ds(0, count)], hss)

    finish(vrecv.at[pl.ds(0, NS - 1)], vrs)

    got = vrecv[...].reshape(NS, 128)
    total = jnp.sum(got, axis=0, keepdims=True)
    got = jnp.where(lane < 32, got, 0.0)
    packed = got[0:16]
    for q in range(1, 4):
        packed += pltpu.roll(got[16 * q : 16 * q + 16], 32 * q, 1)
    row16 = lax.broadcasted_iota(jnp.int32, (16, 128), 0)
    lane16 = lax.broadcasted_iota(jnp.int32, (16, 128), 1)
    spare = jnp.broadcast_to(pltpu.roll(jnp.where((lane1 == 32) | (lane1 == 33), total, 0.0), 64, 1), (16, 128))
    packed = jnp.where((row16 == 15) & (lane16 >= 96), spare, packed)
    psend[...] = packed
    others(lambda peer: remote(psend, precv.at[mp], pss, prs, {"pts": peer}).start())
    precv[mp] = packed
    finish(vsend.at[pl.ds(0, NS - 1)], vss)
    finish(precv.at[pl.ds(0, NP - 1)], prs)
    forward = jnp.sum(precv[...], axis=0)

    def at_lane(x, n):
        return jnp.sum(jnp.where(lax.broadcasted_iota(jnp.int32, x.shape, 1) == n, x, 0.0), axis=1, keepdims=True)

    last = forward[15:16]
    step = [at_lane(total, 34 + r) / (at_lane(last, 96 + r) + at_lane(total, 36 + r)) for r in range(2)]
    spread_out = []
    for part in parts2(forward):
        tiled = lax.dot_general(part, small_v[128:144].astype(bf16), (((0,), (0,)), ((), ())), preferred_element_type=f32)
        tiled = (tiled * small_v[0:128]).astype(bf16)
        spread_out.append(jnp.dot(small_v[304:312, 0:128].astype(bf16), tiled, preferred_element_type=f32)[0:4])
    both = jnp.concatenate(spread_out, axis=0).astype(bf16)
    hi, lo = (jnp.dot(both, idft_2[part], preferred_element_type=f32) for part in range(2))
    signal = hi[0:4] + hi[4:8] + lo[0:4]
    row2 = lax.broadcasted_iota(jnp.int32, (2, NT), 0)
    size = jnp.where(row2 == 0, step[0], step[1])
    for s in range(2):
        image = cov[s] + masks[s] * signal[2 * s : 2 * s + 2]
        out[0, s] = size * direction[s]
        out[1, s] = start[s] - size * image
    finish(precv.at[pl.ds(0, NP - 1)], pss)


def shards(observed, spectra, prior_factor, noise_cov, noise_inv, sensor_block, window_len):
    any_ = pl.BlockSpec(memory_space=pl.ANY)
    dma, vmem = pltpu.SemaphoreType.DMA, pltpu.VMEM
    both = pl.pallas_call(
        kernel,
        out_shape=jax.ShapeDtypeStruct((2, 2, 2, NT), f32),
        in_specs=[any_] * 10,
        out_specs=pl.BlockSpec(memory_space=vmem),
        scratch_shapes=[
            pltpu.SMEM((2,), jnp.int32),
            pltpu.SMEM((2,), jnp.int32),
            vmem((2, 2, NT), f32),
            vmem((NS, 2, FB, 2, PD), bf16),
            vmem((NS * 16, PD), bf16),
            vmem((PD, PD), bf16),
            vmem((TP, NB, NT), bf16),
            vmem((TP, NB, NT), bf16),
            vmem((512, NT), f32),
            vmem((512, NT), f32),
            vmem((2, 512, NT), bf16),
            vmem((2, TP, NT), bf16),
            vmem((NS, 1, 128), f32),
            vmem((NS, 1, 128), f32),
            vmem((NS, 1, 128), f32),
            vmem((NS, 1, 128), f32),
            vmem((16, 128), f32),
            vmem((NP, 16, 128), f32),
            vmem((312, 512), f32),
            dma((9,)),
            dma((4,)),
        ]
        + [dma(())] * 7,
        compiler_params=pltpu.CompilerParams(
            collective_id=0, has_side_effects=True, vmem_limit_bytes=60 << 20
        ),
        cost_estimate=pl.CostEstimate(flops=10**10, bytes_accessed=10**7, transcendentals=0),
    )(
        window_len, sensor_block, observed, spectra, prior_factor,
        noise_inv.transpose(1, 0, 2), noise_cov.transpose(1, 0, 2),
        *tables(),
    )
    return both[0], both[1]


def solution(mesh):
    placed = (
        P("sens", None, None),
        P(None, None, "sens", "pts"),
        P("pts", None),
        P(),
        P(),
        P("sens"),
        P("sens"),
    )
    return jax.shard_map(
        shards,
        mesh=mesh,
        in_specs=placed,
        out_specs=(P("sens", None, None), P("sens", None, None)),
        check_vma=False,
    )
```

time: 117 us -> 97.3 us (0.83)
  local copies, waits for them, and re-layouts: 14 us -> 1.32 us
  Pallas kernels: 101 us -> 95.1 us
    unnamed x26 -> x0, local copies, waits for them, and re-layouts: 6.38 us -> none
    pallas_call x1, Pallas kernels: 101 us -> 95.1 us  [shards(): pl.pallas_call(kernel, out_shape=jax.ShapeDtypeStruct((2, 2, 2, NT), f32)...]
    reshape x2 -> x0, local copies, waits for them, and re-layouts: 5.31 us -> none  [shards(): kx.reshape(2, NC, FB, 2, PD).transpose(1, 0, 2, 3, 4).reshape(NC, 16, PD)]
    pad x1 -> x0, local copies, waits for them, and re-layouts: 2.32 us -> none  [shards(): kx = jnp.pad(spectra, ((0, 0), (0, NC * FB - F), (0, 0), (0, 0)))]
    squeeze x0 -> x1, local copies, waits for them, and re-layouts: none -> 1.32 us  [shards(): return (both[0], both[1])]
where the time goes in v3:
time: 97.3 us; the launch traced here: 97.1 us
  Pallas kernels  95.1 us (98%)
  local copies, waits for them, and re-layouts  1.32 us (1%)
    pallas_call x1, Pallas kernels, shards(): pl.pallas_call(kernel, out_shape=jax.ShapeDtypeStruct((2, 2, 2, NT), f32)...  95.1 us

profile of v3, /device:TPU:1, one launch (start us, length us, event | category | flops | bytes accessed | tf_op | source)
XLA Modules:
  0.0 97.1 jit_solution(4278731515255068883)
XLA Ops:
  0.6 95.1 %shard_map.113 = f32[2,2,2,420]{3,2,1,0:T(2,128)} custom-call(s32[2]{0:T(128)} %wl_any.1, s32[2]{0:T(128)} %sb_any.1, f32[2,2,420]{2,1,0:T(2,128)} %obs_any.1, bf16[2,211,2,768]{3,2,1,0:T(2,128)(2,1)} %kx.1, bf16[768,768]{1,0:T(8,128)(2,1)} %prior.1, bf16[420,4,420]{2,1,0:T(4,128)(2,1)} %bitcast.6, bf16[420,4,420]{2,1,0:T(4,128)(2,1)} %bitcast.7, ...), custom_call_target="tpu_custom_call" | custom-call | flops 10000000000 | bytes 10000000 | tf_op jit(solution)/shard_map/pallas_call | solution.py:338
  95.8 1.3 %slice_bitcast_fusion = (f32[2,2,420]{2,1,0:T(2,128)}, f32[2,2,420]{2,1,0:T(2,128)}) fusion(f32[2,2,2,420]{3,2,1,0:T(2,128)} %shard_map.113), kind=kLoop, calls=%fused_computation | loop fusion | bytes 26880 | tf_op jit(solution)/shard_map/squeeze | solution.py:376

commit v4 on v3

--- a/solution.py
+++ b/solution.py
@@ -105,28 +105,19 @@
     my_chunk = chunk_of(me)
     at_x, in_z, in_core = (me // 2) % 8, me // 16, me % 2
     at_z = [((in_z + dz) % 4) * 16 for dz in range(4)]
-    at_core = [in_core, 1 - in_core]
-
-    def partners(body, low=0, high=4):
+
+    def partners(body, low=0, high=16):
         @pl.loop(low, high)
-        def _(t):
-            for back_x in range(2):
-                step = t if back_x == 0 else jnp.where(t == 0, 4, 8 - t)
-                x = ((at_x + step) % 8) * 2
-                there = jnp.where(t == 0, back_x, 1 - back_x) * 8 + t * 16
-                for dz in range(4):
-                    for dc in range(2):
-                        todo = functools.partial(
-                            body,
-                            at_z[dz] + x + at_core[dc],
-                            t * 16 + back_x * 8 + dz * 2 + dc,
-                            there + (-dz % 4) * 2 + dc,
-                            t,
-                        )
-                        if back_x == dz == dc == 0:
-                            pl.when(t != 0)(todo)
-                        else:
-                            todo()
+        def _(u):
+            dc, dx = u // 8, u % 8
+            base = ((at_x + dx) % 8) * 2 + (in_core + dc) % 2
+            here = dc * 32 + ((8 - dx) % 8) * 4
+            for dz in range(4):
+                todo = functools.partial(body, at_z[dz] + base, here + -dz % 4, u * 4 + dz, u // 4)
+                if dz == 0:
+                    pl.when(u != 0)(todo)
+                else:
+                    todo()
 
     def others(body):
         for k in range(1, NP):
@@ -173,7 +164,7 @@
             first = first_bin(chunk_of(peer))
             remote(kx.at[:, pl.ds(first, FB)], raw.at[there], ksend, krecv.at[t], {"sens": peer}).start()
 
-    partners(send_bins, 0, 3)
+    partners(send_bins, 0, 10)
 
     for copy in locals_[:4]:
         copy.wait()
@@ -226,7 +217,7 @@
             remote(hsend.at[peer], hrecv.at[there], hss, hrs, {"sens": peer}).start()
 
     partners(send_hat)
-    partners(send_bins, 3, 4)
+    partners(send_bins, 10, 16)
     hrecv[0] = hsend[me]
 
     locals_[5].wait()

time: 97.3 us -> 83.7 us (0.86)
  Pallas kernels: 95.1 us -> 81 us
    pallas_call x1, Pallas kernels: 95.1 us -> 81 us  [shards(): pl.pallas_call(kernel, out_shape=jax.ShapeDtypeStruct((2, 2, 2, NT), f32)...]
where the time goes in v4:
time: 83.7 us; the launch traced here: 83 us
  Pallas kernels  81 us (97%)
  local copies, waits for them, and re-layouts  1.32 us (2%)
    pallas_call x1, Pallas kernels, shards(): pl.pallas_call(kernel, out_shape=jax.ShapeDtypeStruct((2, 2, 2, NT), f32)...  81 us

profile of v4, /device:TPU:1, one launch (start us, length us, event | category | flops | bytes accessed | tf_op | source)
XLA Modules:
  0.0 83.0 jit_solution(16924636875872152373)
XLA Ops:
  0.6 81.0 %shard_map.113 = f32[2,2,2,420]{3,2,1,0:T(2,128)} custom-call(s32[2]{0:T(128)} %wl_any.1, s32[2]{0:T(128)} %sb_any.1, f32[2,2,420]{2,1,0:T(2,128)} %obs_any.1, bf16[2,211,2,768]{3,2,1,0:T(2,128)(2,1)} %kx.1, bf16[768,768]{1,0:T(8,128)(2,1)} %prior.1, bf16[420,4,420]{2,1,0:T(4,128)(2,1)} %bitcast.6, bf16[420,4,420]{2,1,0:T(4,128)(2,1)} %bitcast.7, ...), custom_call_target="tpu_custom_call" | custom-call | flops 10000000000 | bytes 10000000 | tf_op jit(solution)/shard_map/pallas_call | solution.py:329
  81.6 1.3 %slice_bitcast_fusion = (f32[2,2,420]{2,1,0:T(2,128)}, f32[2,2,420]{2,1,0:T(2,128)}) fusion(f32[2,2,2,420]{3,2,1,0:T(2,128)} %shard_map.113), kind=kLoop, calls=%fused_computation | loop fusion | bytes 26880 | tf_op jit(solution)/shard_map/squeeze | solution.py:367

commit v5 on v4

--- a/solution.py
+++ b/solution.py
@@ -69,13 +69,14 @@
     fold = np.zeros((8, 128))
     for row in range(128):
         fold[row % 4, row] = 1
-    small = np.zeros((312, 512))
-    small[0:128] = pick
-    small[128:144] = rep
-    small[144:160, :128] = gt.T
-    small[160:176, :128] = mask
-    small[176:304, :16] = gt
-    small[304:312, :128] = fold
+    small = np.zeros((440, 512))
+    small[0:128] = small[128:256] = pick
+    small[256:272] = rep
+    small[272:288, :128] = gt.T
+    small[288:304, :128] = mask
+    small[304:432, :16] = gt
+    small[432:436, 0:128] = small[436:440, 128:256] = fold[0:4]
+    inv = np.pad(inv, ((0, 0), (0, 512 - NT)))
     return [a.astype(np.float32) for a in (fwd, inv, small)]
 
 
@@ -107,17 +108,19 @@
     at_z = [((in_z + dz) % 4) * 16 for dz in range(4)]
 
     def partners(body, low=0, high=16):
-        @pl.loop(low, high)
-        def _(u):
-            dc, dx = u // 8, u % 8
-            base = ((at_x + dx) % 8) * 2 + (in_core + dc) % 2
-            here = dc * 32 + ((8 - dx) % 8) * 4
-            for dz in range(4):
-                todo = functools.partial(body, at_z[dz] + base, here + -dz % 4, u * 4 + dz, u // 4)
-                if dz == 0:
-                    pl.when(u != 0)(todo)
-                else:
-                    todo()
+        @pl.loop(low // 2, high // 2)
+        def _(w):
+            for half in range(2):
+                u = w * 2 + half
+                dc, dx = w // 4, (w % 4) * 2 + half
+                base = ((at_x + dx) % 8) * 2 + (in_core + dc) % 2
+                here = dc * 32 + ((8 - dx) % 8) * 4
+                for dz in range(4):
+                    todo = functools.partial(body, at_z[dz] + base, here + -dz % 4, u * 4 + dz, w // 2)
+                    if dz == half == 0:
+                        pl.when(w != 0)(todo)
+                    else:
+                        todo()
 
     def others(body):
         for k in range(1, NP):
@@ -227,13 +230,15 @@
     curve = sum(jnp.sum(cov[s] * direction[s], axis=1, keepdims=True) for s in range(2))
     for copy in locals_[6:]:
         copy.wait()
-    idft_2[0], idft_2[1] = parts2(idft_v[...])
+    idft_2[:, 0:512], idft_2[:, 512:1024] = parts2(idft_v[...])
+    rep_2 = small_v[256:272].astype(bf16)
+    fold_2 = small_v[432:440, 0:256].astype(bf16)
 
     lane1 = lax.broadcasted_iota(jnp.int32, (1, 128), 1)
     known = jnp.zeros((1, 128), f32)
     for at, value in ((34, inner[0:1]), (35, inner[1:2]), (36, curve[0:1]), (37, curve[1:2])):
         known += jnp.where(lane1 == at, value, 0.0)
-    mask16 = small_v[160:176, 0:128]
+    mask16 = small_v[288:304, 0:128]
 
     @pl.when(mine)
     def _():
@@ -241,21 +246,23 @@
         rows = hrecv[...]
         twice = rows + pltpu.roll(rows.reshape(NS, 128), 32, 1).reshape(NS, 1, 128)
         z = (jnp.broadcast_to(twice, (NS, 16, 128)) * mask16[None]).reshape(NS * 16, 128).astype(bf16)
-        h = nt_dot(small_v[144:160, 0:128].astype(bf16), z).astype(bf16)
-
-        @pl.loop(0, 4)
-        def _(t):
+        h = nt_dot(small_v[272:288, 0:128].astype(bf16), z).astype(bf16)
+
+        adjoint = jnp.zeros((16, PD), f32)
+        for t in range(4):
             finish(raw.at[pl.ds(t * 16, 16)], krecv.at[t])
 
-            @pl.loop(0, 16)
+            @pl.loop(0, 16, unroll=4)
             def _(i):
                 slot = t * 16 + i
                 kk[pl.ds(pl.multiple_of(slot * 16, 16), 16), :] = raw[slot].reshape(16, PD)
 
-        adjoint = jnp.dot(h, kk[...], preferred_element_type=f32).astype(bf16)
+            rows_t = slice(t * 256, t * 256 + 256)
+            adjoint += jnp.dot(h[:, rows_t], kk[rows_t, :], preferred_element_type=f32)
+        adjoint = adjoint.astype(bf16)
         weighted = jnp.dot(adjoint, prior_v[...], preferred_element_type=f32).astype(bf16)
         spread = nt_dot(weighted, prior_v[...]).astype(bf16)
-        spread = jnp.dot(small_v[176:304, 0:16].astype(bf16), spread, preferred_element_type=f32).astype(bf16)
+        spread = jnp.dot(small_v[304:432, 0:16].astype(bf16), spread, preferred_element_type=f32).astype(bf16)
         cross = nt_dot(kk[...], spread)
         folded = (cross.reshape(NS, 16, 128) * mask16[None]).sum(axis=1)
         folded = folded + pltpu.roll(folded, 96, 1)
@@ -306,14 +313,12 @@
 
     last = forward[15:16]
     step = [at_lane(total, 34 + r) / (at_lane(last, 96 + r) + at_lane(total, 36 + r)) for r in range(2)]
-    spread_out = []
-    for part in parts2(forward):
-        tiled = lax.dot_general(part, small_v[128:144].astype(bf16), (((0,), (0,)), ((), ())), preferred_element_type=f32)
-        tiled = (tiled * small_v[0:128]).astype(bf16)
-        spread_out.append(jnp.dot(small_v[304:312, 0:128].astype(bf16), tiled, preferred_element_type=f32)[0:4])
-    both = jnp.concatenate(spread_out, axis=0).astype(bf16)
-    hi, lo = (jnp.dot(both, idft_2[part], preferred_element_type=f32) for part in range(2))
-    signal = hi[0:4] + hi[4:8] + lo[0:4]
+    fine = jnp.concatenate(parts2(forward), axis=1)
+    tiled = lax.dot_general(fine, rep_2, (((0,), (0,)), ((), ())), preferred_element_type=f32)
+    tiled = (tiled * small_v[0:256]).astype(bf16)
+    both = jnp.dot(fold_2, tiled, preferred_element_type=f32).astype(bf16)
+    full = jnp.dot(both, idft_2[...], preferred_element_type=f32)
+    signal = full[0:4, 0:NT] + full[4:8, 0:NT] + full[0:4, 512 : 512 + NT]
     row2 = lax.broadcasted_iota(jnp.int32, (2, NT), 0)
     size = jnp.where(row2 == 0, step[0], step[1])
     for s in range(2):
@@ -324,12 +329,12 @@
 
 
 def shards(observed, spectra, prior_factor, noise_cov, noise_inv, sensor_block, window_len):
-    any_ = pl.BlockSpec(memory_space=pl.ANY)
+    hbm = pl.BlockSpec(memory_space=pltpu.HBM)
     dma, vmem = pltpu.SemaphoreType.DMA, pltpu.VMEM
     both = pl.pallas_call(
         kernel,
         out_shape=jax.ShapeDtypeStruct((2, 2, 2, NT), f32),
-        in_specs=[any_] * 10,
+        in_specs=[hbm] * 10,
         out_specs=pl.BlockSpec(memory_space=vmem),
         scratch_shapes=[
             pltpu.SMEM((2,), jnp.int32),
@@ -341,8 +346,8 @@
             vmem((TP, NB, NT), bf16),
             vmem((TP, NB, NT), bf16),
             vmem((512, NT), f32),
-            vmem((512, NT), f32),
-            vmem((2, 512, NT), bf16),
+            vmem((512, 512), f32),
+            vmem((512, 1024), bf16),
             vmem((2, TP, NT), bf16),
             vmem((NS, 1, 128), f32),
             vmem((NS, 1, 128), f32),
@@ -350,7 +355,7 @@
             vmem((NS, 1, 128), f32),
             vmem((16, 128), f32),
             vmem((NP, 16, 128), f32),
-            vmem((312, 512), f32),
+            vmem((440, 512), f32),
             dma((9,)),
             dma((4,)),
         ]

time: 83.7 us -> 83 us (level)
  no operation moved by 1% of the time
where the time goes in v5:
time: 83 us; the launch traced here: 82.3 us
  Pallas kernels  80.4 us (97%)
  local copies, waits for them, and re-layouts  1.32 us (2%)
    pallas_call x1, Pallas kernels, shards(): pl.pallas_call(kernel, out_shape=jax.ShapeDtypeStruct((2, 2, 2, NT), f32)...  80.4 us

profile of v5, /device:TPU:1, one launch (start us, length us, event | category | flops | bytes accessed | tf_op | source)
XLA Modules:
  0.0 82.3 jit_solution(6783175496719213708)
XLA Ops:
  0.6 80.4 %shard_map.113 = f32[2,2,2,420]{3,2,1,0:T(2,128)} custom-call(s32[2]{0:T(128)} %wl_any.1, s32[2]{0:T(128)} %sb_any.1, f32[2,2,420]{2,1,0:T(2,128)} %obs_any.1, bf16[2,211,2,768]{3,2,1,0:T(2,128)(2,1)} %kx.1, bf16[768,768]{1,0:T(8,128)(2,1)} %prior.1, bf16[420,4,420]{2,1,0:T(4,128)(2,1)} %bitcast.6, bf16[420,4,420]{2,1,0:T(4,128)(2,1)} %bitcast.7, ...), custom_call_target="tpu_custom_call" | custom-call | flops 10000000000 | bytes 10000000 | tf_op jit(solution)/shard_map/pallas_call | solution.py:334
  81.0 1.3 %slice_bitcast_fusion = (f32[2,2,420]{2,1,0:T(2,128)}, f32[2,2,420]{2,1,0:T(2,128)}) fusion(f32[2,2,2,420]{3,2,1,0:T(2,128)} %shard_map.113), kind=kLoop, calls=%fused_computation | loop fusion | bytes 26880 | tf_op jit(solution)/shard_map/squeeze | solution.py:372
